TPU v7x, 32 devices: a whole 2x2x4 slice. The times are simulated.
32 devices in a mesh: segment: 4 (over x, core), dp: 2 (over y), mp: 4 (over z).
Axes of the slice: x: 2, y: 2, z: 4, core: 2. Of those that a mesh axis runs over, the one named last changes fastest.
Arguments:
- encoder_image_states: bfloat16 [2, 32, 8192], P('dp', 'segment'), may hold values from -6 to 6
- frozen_key_value: bfloat16 [4, 8192, 2, 1024], P('segment', 'dp', None, 'mp'), may hold values from -0.0625 to 0.0625
- adapter_down_weight: bfloat16 [4, 8192, 128], P('segment', 'mp'), may hold values from -0.0625 to 0.0625
- adapter_up_weight: bfloat16 [4, 2, 64, 1024], P('segment', None, None, 'mp'), may hold values from -0.75 to 0.75
- queries: bfloat16 [4, 2, 128, 8192], P('segment', 'dp', None, 'mp'), may hold values from -9 to 9
- cotangent: bfloat16 [4, 2, 128, 8192], P('segment', 'dp', None, 'mp'), may hold values from -1.5 to 1.5
- text_token_length: int32 [2], P('dp'), may hold values from 32 to 128
- image_tile_count: int32 [2], P('dp'), may hold values from 1 to 4
Outputs:
- grad_down: bfloat16 [4, 8192, 128], P('segment', 'mp')
- up_gradient: bfloat16 [4, 2, 64, 1024], P('segment', None, None, 'mp')
- grad_image: float32 [2, 32, 8192], P('dp', 'segment')
All inputs are finite; a program needn't handle non-finite values.
Results may differ from a plain program's by a relative error of at most 0.017.
The roundings to bfloat16 on the way count: a program that leaves them out, or rounds other values in their place, can miss the bound.
Values may be sent and summed in bfloat16 or wider, within the bound.
A program may use at most 64 MiB of HBM per device.

v0:
```python
import jax
import jax.numpy as jnp
from jax import lax
from jax.sharding import PartitionSpec as P

HD = 128
TILES = 4


adapter_scale = 2.0
contract_rows = (((0,), (0,)), ((), ()))
contracted_columns = (((1,), (1,)), ((), ()))


def body(
    encoder_image_states,
    frozen_key_value,
    adapter_down_weight,
    adapter_up_weight,
    queries,
    cotangent,
    text_token_length,
    image_tile_count,
):
    samples = encoder_image_states.shape[0]
    model_width = encoder_image_states.shape[2]
    whole_img = lax.all_gather(encoder_image_states, "segment", axis=1, tiled=True)
    image_rows = whole_img.shape[1]
    flat_rows = samples * image_rows
    flat_img = whole_img.reshape(flat_rows, model_width)
    fourth_part = adapter_down_weight.shape[1]
    parallel_index = lax.axis_index("mp")
    image_fourth = lax.dynamic_slice_in_dim(flat_img, parallel_index * fourth_part, fourth_part, 1)
    lowrank_state = adapter_up_weight.shape[2]
    key_value_columns = adapter_up_weight.shape[3]
    lowrank_projection = lax.psum(
        jnp.dot(image_fourth, adapter_down_weight[0], preferred_element_type=jnp.float32), "mp"
    ).astype(jnp.bfloat16)
    adapted_weight = jnp.concatenate(
        [
            jnp.dot(
                lowrank_projection[:, :lowrank_state],
                adapter_up_weight[0, 0],
                preferred_element_type=jnp.float32,
            ),
            jnp.dot(
                lowrank_projection[:, lowrank_state:],
                adapter_up_weight[0, 1],
                preferred_element_type=jnp.float32,
            ),
        ],
        axis=1,
    )
    local_weight = frozen_key_value[0]
    full_weight = lax.all_gather(local_weight, "dp", axis=0, tiled=True).reshape(
        model_width, 2 * key_value_columns
    )
    frozen_output = jnp.dot(flat_img, full_weight, preferred_element_type=jnp.float32)
    key_value_pair = (frozen_output + adapter_scale * adapted_weight).astype(jnp.bfloat16)
    local_heads = queries.shape[3] // HD
    local_kv = key_value_columns // HD
    group_size = local_heads // local_kv
    text_rows = queries.shape[2]
    query_rows = queries[0].reshape(samples, text_rows, local_kv, group_size, HD)
    cot_rows = cotangent[0].reshape(samples, text_rows, local_kv, group_size, HD)
    key_rows = key_value_pair[:, :key_value_columns].reshape(samples, image_rows, local_kv, HD)
    value_rows = key_value_pair[:, key_value_columns:].reshape(samples, image_rows, local_kv, HD)
    key_mask = jnp.arange(image_rows, dtype=jnp.int32)[None, :] < image_tile_count[:, None] * (
        image_rows // TILES
    )
    row_mask = (
        jnp.arange(text_rows, dtype=jnp.int32)[None, :] < text_token_length[:, None]
    ).astype(jnp.float32)
    scores = jnp.einsum(
        "btgrd,bjgd->bgrtj", query_rows, key_rows, preferred_element_type=jnp.float32
    ) * HD ** (-0.5)
    masked = jnp.where(key_mask[:, None, None, None, :], scores, -1e30)
    row_top = jnp.max(masked, axis=-1, keepdims=True)
    shifted = jnp.exp(masked - row_top)
    attention = shifted / jnp.sum(shifted, axis=-1, keepdims=True)
    row_gate = row_mask[:, None, None, :, None]
    kept = attention.astype(jnp.bfloat16) * row_gate.astype(jnp.bfloat16)
    dweights = jnp.einsum(
        "btgrd,bjgd->bgrtj", cot_rows, value_rows, preferred_element_type=jnp.float32
    )
    row_delta = jnp.sum(attention * dweights, axis=-1, keepdims=True)
    dscore = (attention * (dweights - row_delta) * row_gate * HD ** (-0.5)).astype(jnp.bfloat16)
    key_grad = jnp.einsum(
        "bgrtj,btgrd->bjgd", dscore, query_rows, preferred_element_type=jnp.float32
    )
    value_grad = jnp.einsum("bgrtj,btgrd->bjgd", kept, cot_rows, preferred_element_type=jnp.float32)
    kv_grad = jnp.concatenate(
        [
            key_grad.reshape(flat_rows, key_value_columns),
            value_grad.reshape(flat_rows, key_value_columns),
        ],
        axis=1,
    ).astype(jnp.bfloat16)
    backward_piece = adapter_scale * jnp.concatenate(
        [
            lax.dot_general(
                kv_grad[:, :key_value_columns],
                adapter_up_weight[0, 0],
                contracted_columns,
                preferred_element_type=jnp.float32,
            ),
            lax.dot_general(
                kv_grad[:, key_value_columns:],
                adapter_up_weight[0, 1],
                contracted_columns,
                preferred_element_type=jnp.float32,
            ),
        ],
        axis=1,
    )
    backward_lowrank = lax.psum(backward_piece, "mp").astype(jnp.bfloat16)
    up_gradient = adapter_scale * jnp.stack(
        [
            lax.dot_general(
                lowrank_projection[:, :lowrank_state],
                kv_grad[:, :key_value_columns],
                contract_rows,
                preferred_element_type=jnp.float32,
            ),
            lax.dot_general(
                lowrank_projection[:, lowrank_state:],
                kv_grad[:, key_value_columns:],
                contract_rows,
                preferred_element_type=jnp.float32,
            ),
        ]
    )
    grad_down = lax.dot_general(
        image_fourth, backward_lowrank, contract_rows, preferred_element_type=jnp.float32
    )
    down_sum, up_sum = lax.psum((grad_down, up_gradient), "dp")
    image_gradient_total = lax.dot_general(
        kv_grad, full_weight, contracted_columns, preferred_element_type=jnp.float32
    )
    adapter_portion = lax.dot_general(
        backward_lowrank,
        adapter_down_weight[0],
        contracted_columns,
        preferred_element_type=jnp.float32,
    )
    current_layer = lax.dynamic_slice_in_dim(
        image_gradient_total, parallel_index * fourth_part, fourth_part, 1
    )
    image_gradient_total = lax.dynamic_update_slice_in_dim(
        image_gradient_total, current_layer + adapter_portion, parallel_index * fourth_part, 1
    )
    image_gradient_total = image_gradient_total.reshape(samples, image_rows, model_width)
    shared_sum = lax.psum_scatter(image_gradient_total, "segment", scatter_dimension=1, tiled=True)
    result = lax.psum(shared_sum, "mp")
    return (down_sum.astype(jnp.bfloat16)[None], up_sum.astype(jnp.bfloat16)[None], result)


def solution(mesh):
    in_specs = (
        P("dp", "segment", None),
        P("segment", "dp", None, "mp"),
        P("segment", "mp", None),
        P("segment", None, None, "mp"),
        P("segment", "dp", None, "mp"),
        P("segment", "dp", None, "mp"),
        P("dp"),
        P("dp"),
    )
    out_specs = (P("segment", "mp", None), P("segment", None, None, "mp"), P("dp", "segment", None))
    return jax.shard_map(body, mesh=mesh, in_specs=in_specs, out_specs=out_specs, check_vma=False)
```

profile of v0, /device:TPU:0, one launch (start us, length us, event | category | flops | bytes accessed | tf_op | source)
XLA Modules:
  0.0 225.2 jit_solution(8290395179214576090)
XLA Ops:
  7.2 0.7 all-gather.3.cloned.1.call-update
  9.3 1.1 copy.43
  10.4 1.1 copy.44
  11.6 8.8 %all_gather.6 = bf16[1,32,8192]{2,1,0:T(8,128)(2,1)S(1)} all-gather(bf16[1,8,8192]{2,1,0:T(8,128)(2,1)} %param.8), channel_id=1, replica_groups=mesh['segment'=4,'dp'=2,'mp'=4] {'segment'}, dimensions={1}, use_global_device_ids=true | all-gather | bytes 655360 | tf_op jit(solution)/shard_map/all_gather | solution.py:27
  20.6 19.0 %psum.35 = bf16[32,128]{1,0:T(8,128)(2,1)S(1)} all-reduce(f32[32,128]{1,0:T(8,128)S(1)} %fusion.11), channel_id=1, replica_groups=mesh['segment'=4,'dp'=2,'mp'=4] {'mp'}, use_global_device_ids=true, to_apply=%region_0.0 | all-reduce | flops 4096 | bytes 24576 | tf_op jit(solution)/shard_map/psum | solution.py:36
  39.6 1.0 fusion.40
  40.6 0.9 fusion.44
  41.5 74.8 %all-gather.3.cloned.1.call-done = bf16[1,8192,2,256]{3,2,0,1:T(2,128)(2,1)} async-done(((bf16[1,4096,2,256]{3,2,0,1:T(2,128)(2,1)}), bf16[1,8192,2,256]{3,2,0,1:T(2,128)(2,1)}) %all-gather.3.cloned.1.call-update) | async-done | bytes 8388624 | tf_op jit(solution)/shard_map/all_gather | solution.py:55
  116.3 8.0 %copy.42 = bf16[1024,8,2,256]{3,1,2,0:T(8,128)(2,1)} copy(bf16[1024,8,2,256]{3,2,1,0:T(2,128)(2,1)} %bitcast.122) | data formatting | bytes 16777216
  124.3 4.9 %fusion.5 = bf16[32,512]{1,0:T(8,128)(2,1)S(1)} fusion(bf16[8192,512]{1,0:T(8,128)(2,1)} %bitcast.120, bf16[1,32,8192]{2,1,0:T(8,128)(2,1)S(1)} %all_gather.6, f32[32,256]{1,0:T(8,128)S(1)} %fusion.40, f32[32,256]{1,0:T(8,128)S(1)} %fusion.44), kind=kOutput, calls=%fused_computation.11 | convolution fusion | flops 268500992 | bytes 9011200 | tf_op jit(solution)/shard_map/dot_general | solution.py:58
  129.3 0.3 fusion.66
  129.6 0.2 fusion.8
  130.1 0.3 multiply_reduce_fusion
  130.4 0.3 fusion.9
  130.9 18.7 %psum.36 = bf16[32,128]{1,0:T(8,128)(2,1)S(1)} all-reduce(f32[32,128]{1,0:T(8,128)S(1)} %maximum_multiply_fusion.2), channel_id=1, replica_groups=mesh['segment'=4,'dp'=2,'mp'=4] {'mp'}, use_global_device_ids=true, to_apply=%region_4.5 | all-reduce | flops 4096 | bytes 24576 | tf_op jit(solution)/shard_map/psum | solution.py:116
  149.6 5.9 %fusion.34 = f32[32,8192]{1,0:T(8,128)S(1)} fusion(bf16[8192,512]{1,0:T(8,128)(2,1)} %bitcast.121, bf16[32,256]{1,0:T(8,128)(2,1)S(1)} %bitcast.137, bf16[32,256]{1,0:T(8,128)(2,1)S(1)} %bitcast.138), kind=kOutput, calls=%fused_computation.48 | convolution fusion | flops 268500992 | bytes 9469952 | tf_op jit(solution)/shard_map/dot_general | solution.py:137
  155.6 0.3 fusion.1
  155.9 1.0 copy-done.1
  157.2 0.2 convolution_bitcast_fusion.1
  157.4 0.3 fusion.23
  157.8 21.4 %reduce-scatter.2.cloned.1.call-done = f32[1,8,8192]{2,1,0:T(8,128)} async-done(((f32[1,32,8192]{2,1,0:T(8,128)}), f32[1,8,8192]{2,1,0:T(8,128)}) %reduce-scatter.2.cloned.1.call-update) | async-done | bytes 262160 | tf_op jit(solution)/shard_map/reduce_scatter | solution.py:153
  179.2 32.5 %all-reduce.5 = (bf16[2048,128]{1,0:T(8,128)(2,1)}, bf16[2,64,256]{2,1,0:T(8,128)(2,1)}) all-reduce(f32[2048,128]{1,0:T(8,128)S(1)} %fusion.23, f32[2,64,256]{2,1,0:T(8,128)S(1)} %maximum_multiply_fusion), channel_id=1, replica_groups=mesh['segment'=4,'dp'=2,'mp'=4] {'dp'}, use_global_device_ids=true, to_apply=%region_5.6 | all-reduce | flops 294912 | bytes 1769472 | tf_op jit(solution)/shard_map/psum | solution.py:136
  211.7 5.3 %all-reduce.4.cloned.1.call-done = f32[1,8,8192]{2,1,0:T(8,128)} async-done(((f32[1,8,8192]{2,1,0:T(8,128)}), f32[1,8,8192]{2,1,0:T(8,128)}) %all-reduce.4.cloned.1.call-update) | async-done | bytes 262160 | tf_op jit(solution)/shard_map/psum | solution.py:154
  217.0 1.7 copy.83
  (27 shorter events, 1.1 us)
Async XLA Ops:
  7.2 13.2 %copy-start = (bf16[1,2048,128]{2,1,0:T(8,128)(2,1)S(1)}, bf16[1,2048,128]{2,1,0:T(8,128)(2,1)}, u32[]{:S(2)}) copy-start(bf16[1,2048,128]{2,1,0:T(8,128)(2,1)} %param.10) | copy-start | bytes 1572868
  7.2 109.1 %all-gather.3.cloned.1.call-start = ((), (), s32[]{:S(2)}) async-start(), calls=%async_computation.3 | async-start | bytes 12582912 | tf_op jit(solution)/shard_map/all_gather | solution.py:55
  7.9 171.3 %reduce-scatter.2.cloned.1.call-start = ((), (), s32[]{:S(2)}) async-start(), calls=%async_computation.1 | async-start | bytes 1310720 | tf_op jit(solution)/shard_map/reduce_scatter | solution.py:153
  124.3 5.6 %copy-start.2 = (bf16[1,2,64,256]{3,2,1,0:T(8,128)(2,1)S(1)}, bf16[1,2,64,256]{3,2,1,0:T(8,128)(2,1)}, u32[]{:S(2)}) copy-start(bf16[1,2,64,256]{3,2,1,0:T(8,128)(2,1)} %param.11) | copy-start | bytes 196612
  155.9 1.0 copy-start.1
  156.9 60.1 %all-reduce.4.cloned.1.call-start = ((), (), s32[]{:S(2)}) async-start(), calls=%async_computation.2 | async-start | bytes 524288 | tf_op jit(solution)/shard_map/psum | solution.py:154
Sparse Core Ops, SparseCore 0:
  9.6 106.6 all-gather.2
  157.1 22.1 reduce-scatter.1
  181.7 35.3 all-reduce.3
where the time goes:
time: 226 us; the launch traced here: 225 us
  waiting for transfers between devices  102 us (45%)
  blocking collectives  79.1 us (35%)
  matrix products  15.3 us (7%)
  between operations  15.2 us (7%)
  local copies, waits for them, and re-layouts  13.1 us (6%)
    all_gather x1, waiting for transfers between devices, body(): lax.all_gather(local_weight, 'dp', axis=0, tiled=True)  74.8 us
    psum x1, blocking collectives, body(): down_sum, up_sum = lax.psum((grad_down, up_gradient), 'dp')  32.5 us
    reduce_scatter x1, waiting for transfers between devices, body(): lax.psum_scatter(image_gradient_total, 'segment', scatter_dimension=1, ti...  21.4 us
    psum x1, blocking collectives, body(): lax.psum(jnp.dot(image_fourth, adapter_down_weight[0], preferred_element_...  19 us
    psum x1, blocking collectives, body(): backward_lowrank = lax.psum(backward_piece, 'mp').astype(jnp.bfloat16)  18.7 us
    unnamed x13, local copies, waits for them, and re-layouts  13.1 us
    all_gather x1, blocking collectives, body(): lax.all_gather(encoder_image_states, 'segment', axis=1, tiled=True)  8.83 us
    dot_general x1, matrix products, body(): lax.dot_general(kv_grad, full_weight, contracted_columns, preferred_eleme...  5.9 us
  transfers between devices with their start and end apart: 3, of which 3 were waited for; matrix products, arithmetic and copies ran while one was open for 2% of the time, Pallas kernels for 0%

commit v1 on v0

v1 whole, which is shorter than its diff:
```python
import functools

import jax
import jax.numpy as jnp
from jax import lax
from jax.experimental import pallas as pl
from jax.experimental.pallas import tpu as pltpu
from jax.sharding import PartitionSpec as P

HD = 128
TILES = 4
ADAPTER_SCALE = 2.0
F32 = jnp.float32
BF16 = jnp.bfloat16
NN = (((1,), (0,)), ((), ()))
NT = (((1,), (1,)), ((), ()))
TN = (((0,), (0,)), ((), ()))


def dot(a, b, dims):
    return lax.dot_general(a, b, dims, preferred_element_type=F32)


def flip(index, bit):
    return index + bit - 2 * bit * lax.rem(lax.div(index, bit), 2)


def bits_down(n):
    bits = []
    while n > 1:
        n //= 2
        bits.append(n)
    return bits


def kernel(
    sizes,
    len_ref, tiles_ref, img_ref, up_ref, w_hbm, a_hbm, q_hbm, c_hbm,
    gdown_ref, gup_ref, gimg_ref,
    w, a, q, c, x, xh, low_p, low_r, kv_p, kv_r, dkv_own, dkv, back_p, back_r,
    g, zs, zr, fin, fr, load_sem, send_sem, recv_sem, *halves,
):
    S, D, M = sizes
    s, d, m = lax.axis_index("segment"), lax.axis_index("dp"), lax.axis_index("mp")
    rows_loc, width = img_ref.shape
    nb = S * D
    rows = nb * rows_loc
    srows = S * rows_loc
    cw = w.shape[0]
    kvc = w.shape[1] // 2
    qw = a.shape[0]
    zw = cw // M
    s_bits, d_bits = bits_down(S), bits_down(D)

    loads = [
        pltpu.make_async_copy(src, dst, load_sem.at[i])
        for i, (src, dst) in enumerate([(w_hbm, w), (a_hbm, a), (q_hbm, q), (c_hbm, c)])
    ]
    for load in loads:
        load.start()

    barrier = pltpu.get_barrier_semaphore()
    peers = [(flip(s, b), d, m) for b in s_bits]
    for i in range(D):
        for j in range(M):
            if i or j:
                peers.append((s, lax.rem(d + i, D), lax.rem(m + j, M)))
    for peer in peers:
        pl.semaphore_signal(barrier, inc=1, device_id=peer, device_id_type=pl.DeviceIdType.MESH)
    pl.semaphore_wait(barrier, len(peers))

    started = []

    def send(src, dst, peer):
        k = len(started)
        copy = pltpu.make_async_remote_copy(
            src_ref=src, dst_ref=dst, send_sem=send_sem.at[k], recv_sem=recv_sem.at[k],
            device_id=peer, device_id_type=pl.DeviceIdType.MESH,
        )
        copy.start()
        started.append(copy)
        return copy

    steps = [("d", b) for b in d_bits] + [("s", b) for b in s_bits]

    def across(step, at):
        kind, b = step
        return (at[0], flip(at[1], b)) if kind == "d" else (flip(at[0], b), at[1])

    me = (s, d)
    held = [[] for _ in steps]
    for k, step in enumerate(steps):
        to = across(step, me)
        held[k].append((send(img_ref, x.at[d * S + s], (*to, m)), across(step, me)))
    x[d * S + s] = img_ref[...]
    for k in range(len(steps)):
        for copy, at in list(held[k]):
            copy.wait_recv()
            slot = x.at[at[1] * S + at[0]]
            for later in range(k + 1, len(steps)):
                to = across(steps[later], me)
                held[later].append((send(slot, slot, (*to, m)), across(steps[later], at)))

    ukk = jnp.concatenate([up_ref[0], jnp.zeros_like(up_ref[0])], axis=0)
    uvv = jnp.concatenate([jnp.zeros_like(up_ref[1]), up_ref[1]], axis=0)

    loads[1].wait()
    xq = x[:, :, pl.ds(pl.multiple_of(m * qw, 128), qw)].astype(F32).reshape(rows, qw).astype(BF16)
    low_p[...] = dot(xq, a[...], NN)
    low_c = [
        send(low_p, low_r.at[m], (s, d, lax.rem(m + j, M))) for j in range(1, M)
    ]
    low_r[m] = low_p[...]

    xh[...] = (
        x[:, :, pl.ds(pl.multiple_of(d * cw, 128), cw)].astype(F32).reshape(rows, cw).astype(BF16)
    )
    loads[0].wait()
    kv_p[...] = dot(xh[...], w[...], NN).reshape(kv_p.shape)
    kv_c = [
        send(kv_p.at[lax.rem(d + i, D)], kv_r.at[d], (s, lax.rem(d + i, D), m))
        for i in range(1, D)
    ]
    kv_r[d] = kv_p[d]
    for copy in low_c:
        copy.wait_recv()
    low = jnp.sum(low_r[...], axis=0).astype(BF16)
    fin_low = low.astype(F32).reshape(D, srows, low.shape[1])
    low_own = jnp.zeros((srows, low.shape[1]), F32)
    for i in range(D):
        low_own = jnp.where(d == i, fin_low[i], low_own)
    low_own = low_own.astype(BF16)
    adapted = jnp.concatenate([dot(low_own, ukk, NN), dot(low_own, uvv, NN)], axis=1)
    for copy in kv_c:
        copy.wait_recv()
    kv = (jnp.sum(kv_r[...], axis=0) + ADAPTER_SCALE * adapted).astype(BF16)

    loads[2].wait()
    loads[3].wait()
    text = q.shape[0]
    heads = q.shape[1] // HD
    kv_heads = kvc // HD
    group = heads // kv_heads
    cols = group * text
    live = (
        lax.rem(lax.broadcasted_iota(jnp.int32, (1, cols), 1), text) < len_ref[0]
    ).astype(F32)
    valid = lax.broadcasted_iota(jnp.int32, (srows, 1), 0) < tiles_ref[0] * (srows // TILES)
    for h in range(kv_heads):
        qs = jnp.concatenate(
            [q[:, (h * group + r) * HD : (h * group + r + 1) * HD] for r in range(group)], axis=0
        )
        cs = jnp.concatenate(
            [c[:, (h * group + r) * HD : (h * group + r + 1) * HD] for r in range(group)], axis=0
        )
        keys = kv[:, h * HD : (h + 1) * HD]
        vals = kv[:, kvc + h * HD : kvc + (h + 1) * HD]
        scores = jnp.where(valid, dot(keys, qs, NT) * HD ** (-0.5), -1e30)
        shifted = jnp.exp(scores - jnp.max(scores, axis=0, keepdims=True))
        att = shifted / jnp.sum(shifted, axis=0, keepdims=True)
        kept = (att.astype(BF16).astype(F32) * live).astype(BF16)
        dp = dot(vals, cs, NT)
        delta = jnp.sum(att * dp, axis=0, keepdims=True)
        ds = (att * (dp - delta) * live * HD ** (-0.5)).astype(BF16)
        dkv_own[:, h * HD : (h + 1) * HD] = dot(ds, qs, NN).astype(BF16)
        dkv_own[:, kvc + h * HD : kvc + (h + 1) * HD] = dot(kept, cs, NN).astype(BF16)

    dkv_c = [
        send(dkv_own, dkv.at[d], (s, lax.rem(d + i, D), m)) for i in range(1, D)
    ]
    dkv[d] = dkv_own[...]
    for copy in dkv_c:
        copy.wait_recv()
    dall = dkv[...].reshape(rows, 2 * kvc)

    back_p[...] = ADAPTER_SCALE * (dot(dall[:, :kvc], ukk, NT) + dot(dall[:, kvc:], uvv, NT))
    back_c = [
        send(back_p, back_r.at[m], (s, d, lax.rem(m + j, M))) for j in range(1, M)
    ]
    back_r[m] = back_p[...]

    step = min(cw, 1024)
    for j in range(0, cw, step):
        g[:, :, j : j + step] = dot(dall, w[j : j + step, :], NT).reshape(nb, rows_loc, step)

    for copy in back_c:
        copy.wait_recv()
    back = jnp.sum(back_r[...], axis=0).astype(BF16)

    if cw >= qw:
        @pl.when(lax.div(m, cw // qw) == d)
        def _():
            at = pl.ds(pl.multiple_of(lax.rem(m, cw // qw) * qw, 128), qw)
            g[:, :, at] = g[:, :, at] + dot(back, a[...], NT).reshape(nb, rows_loc, qw)
    else:
        @pl.when(lax.div(d, qw // cw) == m)
        def _():
            at = pl.ds(pl.multiple_of(lax.rem(d, qw // cw) * cw, 128), cw)
            g[...] = g[...] + dot(back, a[at, :], NT).reshape(nb, rows_loc, cw)


    def adapters():
        up = jnp.concatenate(
            [
                dot(low, dall[:, :kvc], TN)[: low.shape[1] // 2],
                dot(low, dall[:, kvc:], TN)[low.shape[1] // 2 :],
            ],
            axis=0,
        )
        gup_ref[...] = (ADAPTER_SCALE * up).astype(BF16).reshape(gup_ref.shape)

    def down():
        xq2 = (
            x[:, :, pl.ds(pl.multiple_of(m * qw, 128), qw)]
            .astype(F32).reshape(rows, qw).astype(BF16)
        )
        gdown_ref[...] = dot(xq2, back, TN).astype(BF16)

    beside = [adapters, down]
    for n, b in enumerate(reversed(s_bits)):
        out_buf, in_buf = halves[2 * n], halves[2 * n + 1]
        count = S // (2 * b)
        mine = lax.rem(lax.div(s, b), 2)
        base = lax.rem(s, b)
        for i in range(D):
            for t in range(count):
                at = i * S + base + b * (1 - mine) + 2 * b * t
                out_buf[i * count + t] = g[at].astype(BF16)
        copy = send(out_buf, in_buf, (flip(s, b), d, m))
        if beside:
            beside.pop(0)()
        copy.wait_recv()
        for i in range(D):
            for t in range(count):
                at = i * S + base + b * mine + 2 * b * t
                g[at] = g[at] + in_buf[i * count + t].astype(F32)
    for work in beside:
        work()

    for j in range(1, M):
        to = lax.rem(m + j, M)
        for i in range(D):
            zs[j - 1, i] = g[i * S + s, :, pl.ds(pl.multiple_of(to * zw, 128), zw)].astype(BF16)
    z_c = [
        send(zs.at[j - 1], zr.at[j - 1], (s, d, lax.rem(m + j, M))) for j in range(1, M)
    ]
    for copy in z_c:
        copy.wait_recv()
    for i in range(D):
        total = g[i * S + s, :, pl.ds(pl.multiple_of(m * zw, 128), zw)]
        for j in range(M - 1):
            total = total + zr[j, i].astype(F32)
        fin[i] = total.astype(BF16)
    f_c = []
    for i in range(D):
        for j in range(M):
            if i or j:
                to = lax.rem(d + i, D)
                f_c.append(send(fin.at[to], fr.at[d * M + m], (s, to, lax.rem(m + j, M))))
    fr[d * M + m] = fin[d]
    for copy in f_c:
        copy.wait_recv()
    for i in range(D * M):
        gimg_ref[:, i * zw : (i + 1) * zw] = fr[i].astype(F32)
    for copy in started:
        copy.wait_send()


def body(
    encoder_image_states,
    frozen_key_value,
    adapter_down_weight,
    adapter_up_weight,
    queries,
    cotangent,
    text_token_length,
    image_tile_count,
    *,
    sizes,
):
    S, D, M = sizes
    rows_loc, width = encoder_image_states.shape[1:]
    cw, kvc = frozen_key_value.shape[1], frozen_key_value.shape[3]
    qw, ranks = adapter_down_weight.shape[1:]
    text, qcols = queries.shape[2:]
    nb = S * D
    rows, srows = nb * rows_loc, S * rows_loc
    zw = cw // M
    vmem = pl.BlockSpec(memory_space=pltpu.VMEM)
    smem = pl.BlockSpec(memory_space=pltpu.SMEM)
    hbm = pl.BlockSpec(memory_space=pl.ANY)
    halves = []
    bits = bits_down(S)
    for b in reversed(bits):
        halves += [pltpu.VMEM((D * S // (2 * b), rows_loc, cw), BF16)] * 2
    sends = (nb - 1) + 3 * (M - 1) + 2 * (D - 1) + len(bits) + (D * M - 1)
    down, up, image = pl.pallas_call(
        functools.partial(kernel, sizes),
        out_shape=(
            jax.ShapeDtypeStruct((qw, ranks), BF16),
            jax.ShapeDtypeStruct(adapter_up_weight.shape[1:], BF16),
            jax.ShapeDtypeStruct((rows_loc, width), F32),
        ),
        in_specs=[smem, smem, vmem, vmem, hbm, hbm, hbm, hbm],
        out_specs=(vmem, vmem, vmem),
        scratch_shapes=[
            pltpu.VMEM((cw, 2 * kvc), BF16),
            pltpu.VMEM((qw, ranks), BF16),
            pltpu.VMEM((text, qcols), BF16),
            pltpu.VMEM((text, qcols), BF16),
            pltpu.VMEM((nb, rows_loc, width), BF16),
            pltpu.VMEM((rows, cw), BF16),
            pltpu.VMEM((rows, ranks), F32),
            pltpu.VMEM((M, rows, ranks), F32),
            pltpu.VMEM((D, srows, 2 * kvc), F32),
            pltpu.VMEM((D, srows, 2 * kvc), F32),
            pltpu.VMEM((srows, 2 * kvc), BF16),
            pltpu.VMEM((D, srows, 2 * kvc), BF16),
            pltpu.VMEM((rows, ranks), F32),
            pltpu.VMEM((M, rows, ranks), F32),
            pltpu.VMEM((nb, rows_loc, cw), F32),
            pltpu.VMEM((M - 1, D, rows_loc, zw), BF16),
            pltpu.VMEM((M - 1, D, rows_loc, zw), BF16),
            pltpu.VMEM((D, rows_loc, zw), BF16),
            pltpu.VMEM((D * M, rows_loc, zw), BF16),
            pltpu.SemaphoreType.DMA((4,)),
            pltpu.SemaphoreType.DMA((sends,)),
            pltpu.SemaphoreType.DMA((sends,)),
            *halves,
        ],
        compiler_params=pltpu.CompilerParams(
            collective_id=0, has_side_effects=True, vmem_limit_bytes=58 * 2**20
        ),
    )(
        text_token_length,
        image_tile_count,
        encoder_image_states[0],
        adapter_up_weight[0],
        frozen_key_value[0].reshape(cw, 2 * kvc),
        adapter_down_weight[0],
        queries[0, 0],
        cotangent[0, 0],
    )
    return down[None], up[None], image[None]


def solution(mesh):
    in_specs = (
        P("dp", "segment", None),
        P("segment", "dp", None, "mp"),
        P("segment", "mp", None),
        P("segment", None, None, "mp"),
        P("segment", "dp", None, "mp"),
        P("segment", "dp", None, "mp"),
        P("dp"),
        P("dp"),
    )
    out_specs = (P("segment", "mp", None), P("segment", None, None, "mp"), P("dp", "segment", None))
    sizes = (mesh.shape["segment"], mesh.shape["dp"], mesh.shape["mp"])
    return jax.shard_map(
        functools.partial(body, sizes=sizes),
        mesh=mesh, in_specs=in_specs, out_specs=out_specs, check_vma=False,
    )
```

time: 226 us -> 57 us (0.25)
  waiting for transfers between devices: 102 us -> 0 us
  blocking collectives: 79.1 us -> 0 us
  Pallas kernels: 0 us -> 44.9 us
  matrix products: 15.3 us -> 0 us
  between operations: 15.2 us -> 1.93 us
  local copies, waits for them, and re-layouts: 13.1 us -> 9.87 us
    all_gather x1 -> x0, waiting for transfers between devices: 74.8 us -> none  [body(): lax.all_gather(local_weight, 'dp', axis=0, tiled=True)]
    psum x3 -> x0, blocking collectives: 70.2 us -> none  [the longest x1 32.5 us: body(): down_sum, up_sum = lax.psum((grad_down, up_gradient), 'dp')]
    pallas_call x0 -> x1, Pallas kernels: none -> 44.9 us  [body(): pl.pallas_call(functools.partial(kernel, sizes), out_shape=(jax.ShapeDtyp...]
    reduce_scatter x1 -> x0, waiting for transfers between devices: 21.4 us -> none  [body(): lax.psum_scatter(image_gradient_total, 'segment', scatter_dimension=1, ti...]
    dot_general x15 -> x0, matrix products: 15.3 us -> none  [the longest x1 5.9 us: body(): lax.dot_general(kv_grad, full_weight, contracted_columns, preferred_eleme...]
    all_gather x1 -> x0, blocking collectives: 8.83 us -> none  [body(): lax.all_gather(encoder_image_states, 'segment', axis=1, tiled=True)]
    psum x1 -> x0, waiting for transfers between devices: 5.32 us -> none  [body(): result = lax.psum(shared_sum, 'mp')]
    unnamed x13 -> x4, local copies, waits for them, and re-layouts: 13.1 us -> 9.87 us
  transfers between devices with their start and end apart: 3 -> 0, of which waited for: 3 -> 0; matrix products, arithmetic and copies ran while one was open for 2% -> 0% of each run, Pallas kernels for 0% -> 0%
where the time goes in v1:
time: 57 us; the launch traced here: 56.7 us
  Pallas kernels  44.9 us (79%)
  local copies, waits for them, and re-layouts  9.87 us (17%)
  between operations  1.93 us (3%)
    pallas_call x1, Pallas kernels, body(): pl.pallas_call(functools.partial(kernel, sizes), out_shape=(jax.ShapeDtyp...  44.9 us
    unnamed x4, local copies, waits for them, and re-layouts  9.87 us

profile of v1, /device:TPU:0, one launch (start us, length us, event | category | flops | bytes accessed | tf_op | source)
XLA Modules:
  0.0 56.7 jit_solution(10491043659955116954)
XLA Ops:
  1.9 4.9 %copy.11 = bf16[512,8,2,256]{3,1,2,0:T(8,128)(2,1)} copy(bf16[512,8,2,256]{3,2,1,0:T(2,128)(2,1)} %bitcast.12) | data formatting | bytes 8388608
  6.8 44.9 %shard_map.103 = (bf16[2048,128]{1,0:T(8,128)(2,1)}, bf16[2,64,256]{2,1,0:T(8,128)(2,1)}, f32[8,8192]{1,0:T(8,128)}) custom-call(s32[1]{0:T(128)S(6)} %copy.15.len_ref, s32[1]{0:T(128)S(6)} %copy.16.tiles_ref, bf16[8,8192]{1,0:T(8,128)(2,1)} %bitcast.18, bf16[2,64,256]{2,1,0:T(8,128)(2,1)} %bitcast.19, bf16[4096,512]{1,0:T(8,128)(2,1)} %bitcast.11, ...), custom_call_target="tpu_custom_call" | custom-call | tf_op jit(solution)/shard_map/pallas_call | solution.py:297
  51.7 1.9 %copy.17 = bf16[1,2048,128]{2,1,0:T(8,128)(2,1)} copy(bf16[1,2048,128]{2,1,0:T(8,128)(2,1)} %bitcast.16) | data formatting | bytes 1048576
  53.5 1.5 %copy.18 = bf16[1,2,64,256]{3,2,1,0:T(8,128)(2,1)} copy(bf16[1,2,64,256]{3,2,1,0:T(8,128)(2,1)} %bitcast.20) | data formatting | bytes 131072
  55.0 1.7 %copy.19 = f32[1,8,8192]{2,1,0:T(8,128)} copy(f32[1,8,8192]{2,1,0:T(8,128)} %bitcast.17) | data formatting | bytes 524288

commit v2 on v1

v2 whole, which is shorter than its diff:
```python
import functools

import jax
import jax.numpy as jnp
from jax import lax
from jax.experimental import pallas as pl
from jax.experimental.pallas import tpu as pltpu
from jax.sharding import PartitionSpec as P

HD = 128
TILES = 4
ADAPTER_SCALE = 2.0
F32 = jnp.float32
BF16 = jnp.bfloat16
NN = (((1,), (0,)), ((), ()))
NT = (((1,), (1,)), ((), ()))
TN = (((0,), (0,)), ((), ()))


def dot(a, b, dims):
    return lax.dot_general(a, b, dims, preferred_element_type=F32)


def flip(index, bit):
    return index + bit - 2 * bit * lax.rem(lax.div(index, bit), 2)


def bits_down(n):
    bits = []
    while n > 1:
        n //= 2
        bits.append(n)
    return bits


def kernel(
    sizes, parts,
    len_ref, tiles_ref, img_ref, up_ref, w_hbm, a_hbm, q_hbm, c_hbm,
    gdown_ref, gup_ref, gimg_ref,
    w, a, q, c, xh, xq, low_p, low_r, low_b, kv_p, kv_r, dkv_own, dkv, back_p, back_r,
    g, zs, zr, fin, fr, load_sem, send_sem, recv_sem, *halves,
):
    S, D, M = sizes
    s, d, m = lax.axis_index("segment"), lax.axis_index("dp"), lax.axis_index("mp")
    rows_loc = xh.shape[1]
    nb = S * D
    rows = nb * rows_loc
    srows = S * rows_loc
    cw = w.shape[0]
    kvc = w.shape[1] // 2
    qw = a.shape[0]
    pw = cw // parts
    zw = pw // M
    s_bits, d_bits = bits_down(S), bits_down(D)

    def columns(at, size):
        return pl.ds(pl.multiple_of(at, 128), size)

    loads = [
        pltpu.make_async_copy(src, dst, load_sem.at[i])
        for i, (src, dst) in enumerate(
            [
                (img_ref.at[:, columns(d * cw, cw)], xh.at[d * S + s]),
                (img_ref.at[:, columns(m * qw, qw)], xq.at[d, s]),
                (a_hbm, a),
                (w_hbm, w),
                (q_hbm, q),
                (c_hbm, c),
            ]
        )
    ]
    for load in loads:
        load.start()

    others = [(i, j) for i in range(D) for j in range(M) if i or j]
    barrier = pltpu.get_barrier_semaphore()
    peers = [(flip(s, b), d, m) for b in s_bits]
    peers += [(s, lax.rem(d + i, D), lax.rem(m + j, M)) for i, j in others]
    for peer in peers:
        pl.semaphore_signal(barrier, inc=1, device_id=peer, device_id_type=pl.DeviceIdType.MESH)
    pl.semaphore_wait(barrier, len(peers))

    started = []

    def send(src, dst, peer):
        k = len(started)
        copy = pltpu.make_async_remote_copy(
            src_ref=src, dst_ref=dst, send_sem=send_sem.at[k], recv_sem=recv_sem.at[k],
            device_id=peer, device_id_type=pl.DeviceIdType.MESH,
        )
        copy.start()
        started.append(copy)
        return copy

    steps = [("d", b) for b in d_bits] + [("s", b) for b in s_bits]

    def across(step, at):
        kind, b = step
        return (at[0], flip(at[1], b)) if kind == "d" else (flip(at[0], b), at[1])

    me = (s, d)
    held = [[] for _ in steps]
    for k, step in enumerate(steps):
        to = across(step, me)
        half = img_ref.at[:, columns(to[1] * cw, cw)]
        held[k].append((send(half, xh.at[d * S + s], (*to, m)), "half", to))
        if step[0] == "s":
            quarter = img_ref.at[:, columns(m * qw, qw)]
            held[k].append((send(quarter, xq.at[d, s], (*to, m)), "quarter", to))
    for k in range(len(steps)):
        for copy, kind, at in list(held[k]):
            copy.wait_recv()
            slot = xh.at[at[1] * S + at[0]] if kind == "half" else xq.at[d, at[0]]
            for later in range(k + 1, len(steps)):
                to = across(steps[later], me)
                held[later].append(
                    (send(slot, slot, (*to, m)), kind, across(steps[later], at))
                )

    ukk = jnp.concatenate([up_ref[0], jnp.zeros_like(up_ref[0])], axis=0)
    uvv = jnp.concatenate([jnp.zeros_like(up_ref[1]), up_ref[1]], axis=0)

    loads[0].wait()
    loads[1].wait()
    loads[2].wait()
    mine_q = xq[d].astype(F32).reshape(srows, qw).astype(BF16)
    low_p[...] = dot(mine_q, a[...], NN)
    low_c = [send(low_p, low_r.at[m], (s, d, lax.rem(m + j, M))) for j in range(1, M)]
    low_r[m] = low_p[...]

    xall = xh[...].astype(F32).reshape(rows, cw).astype(BF16)
    loads[3].wait()
    kv_p[...] = dot(xall, w[...], NN).reshape(kv_p.shape)
    samples = [lax.rem(d + i, D) for i in range(1, D)]
    kv_c = [send(kv_p.at[to], kv_r.at[d], (s, to, m)) for to in samples]
    xq_c = [send(xq.at[d], xq.at[d], (s, to, m)) for to in samples]
    kv_r[d] = kv_p[d]
    for copy in low_c:
        copy.wait_recv()
    low_own = jnp.sum(low_r[...], axis=0).astype(BF16)
    low_b[d] = low_own
    lowb_c = [send(low_b.at[d], low_b.at[d], (s, to, m)) for to in samples]
    adapted = jnp.concatenate([dot(low_own, ukk, NN), dot(low_own, uvv, NN)], axis=1)
    for copy in kv_c:
        copy.wait_recv()
    kv = (jnp.sum(kv_r[...], axis=0) + ADAPTER_SCALE * adapted).astype(BF16)

    loads[4].wait()
    loads[5].wait()
    text = q.shape[0]
    heads = q.shape[1] // HD
    kv_heads = kvc // HD
    group = heads // kv_heads
    cols = group * text
    live = (
        lax.rem(lax.broadcasted_iota(jnp.int32, (1, cols), 1), text) < len_ref[0]
    ).astype(F32)
    valid = lax.broadcasted_iota(jnp.int32, (srows, 1), 0) < tiles_ref[0] * (srows // TILES)
    for h in range(kv_heads):
        qs = jnp.concatenate(
            [q[:, (h * group + r) * HD : (h * group + r + 1) * HD] for r in range(group)], axis=0
        )
        cs = jnp.concatenate(
            [c[:, (h * group + r) * HD : (h * group + r + 1) * HD] for r in range(group)], axis=0
        )
        keys = kv[:, h * HD : (h + 1) * HD]
        vals = kv[:, kvc + h * HD : kvc + (h + 1) * HD]
        scores = jnp.where(valid, dot(keys, qs, NT) * HD ** (-0.5), -1e30)
        shifted = jnp.exp(scores - jnp.max(scores, axis=0, keepdims=True))
        att = shifted / jnp.sum(shifted, axis=0, keepdims=True)
        kept = (att.astype(BF16).astype(F32) * live).astype(BF16)
        dp = dot(vals, cs, NT)
        delta = jnp.sum(att * dp, axis=0, keepdims=True)
        ds = (att * (dp - delta) * live * HD ** (-0.5)).astype(BF16)
        dkv_own[:, h * HD : (h + 1) * HD] = dot(ds, qs, NN).astype(BF16)
        dkv_own[:, kvc + h * HD : kvc + (h + 1) * HD] = dot(kept, cs, NN).astype(BF16)

    dkv_c = [send(dkv_own, dkv.at[d], (s, to, m)) for to in samples]
    own = dkv_own[...]
    dkv[d] = own
    back_p[...] = ADAPTER_SCALE * (dot(own[:, :kvc], ukk, NT) + dot(own[:, kvc:], uvv, NT))
    back_c = [
        send(back_p, back_r.at[d, m], (s, lax.rem(d + i, D), lax.rem(m + j, M)))
        for i, j in others
    ]
    back_r[d, m] = back_p[...]
    for copy in dkv_c:
        copy.wait_recv()
    dall = dkv[...].reshape(rows, 2 * kvc)

    step = min(cw, 1024)
    for j in range(0, cw, step):
        g[:, :, j : j + step] = dot(dall, w[j : j + step, :], NT).reshape(nb, rows_loc, step)

    for copy in back_c:
        copy.wait_recv()
    back = jnp.sum(back_r[...], axis=1).reshape(rows, back_r.shape[3]).astype(BF16)

    if cw >= qw:
        @pl.when(lax.div(m, cw // qw) == d)
        def _():
            at = columns(lax.rem(m, cw // qw) * qw, qw)
            g[:, :, at] = g[:, :, at] + dot(back, a[...], NT).reshape(nb, rows_loc, qw)
    else:
        @pl.when(lax.div(d, qw // cw) == m)
        def _():
            at = columns(lax.rem(d, qw // cw) * cw, cw)
            g[...] = g[...] + dot(back, a[at, :], NT).reshape(nb, rows_loc, cw)

    def adapter_up():
        for copy in lowb_c:
            copy.wait_recv()
        low = low_b[...].reshape(rows, low_b.shape[2])
        rank = low.shape[1] // 2
        gup_ref[0] = (ADAPTER_SCALE * dot(low, dall[:, :kvc], TN)[:rank]).astype(BF16)
        gup_ref[1] = (ADAPTER_SCALE * dot(low, dall[:, kvc:], TN)[rank:]).astype(BF16)

    def adapter_down():
        for copy in xq_c:
            copy.wait_recv()
        all_q = xq[...].astype(F32).reshape(rows, qw).astype(BF16)
        gdown_ref[...] = dot(all_q, back, TN).astype(BF16)

    ladder = list(reversed(s_bits))
    flying = {}

    def halve_send(n, p):
        b = ladder[n]
        count = S // (2 * b)
        theirs = lax.rem(s, b) + b * (1 - lax.rem(lax.div(s, b), 2))
        for i in range(D):
            for t in range(count):
                halves[2 * n][p, i * count + t] = g[
                    i * S + theirs + 2 * b * t, :, p * pw : (p + 1) * pw
                ].astype(BF16)
        flying[p] = [send(halves[2 * n].at[p], halves[2 * n + 1].at[p], (flip(s, b), d, m))]

    def halve_take(n, p):
        b = ladder[n]
        count = S // (2 * b)
        ours = lax.rem(s, b) + b * lax.rem(lax.div(s, b), 2)
        flying[p][0].wait_recv()
        for i in range(D):
            for t in range(count):
                at = i * S + ours + 2 * b * t
                g[at, :, p * pw : (p + 1) * pw] = g[at, :, p * pw : (p + 1) * pw] + halves[
                    2 * n + 1
                ][p, i * count + t].astype(F32)

    def group_send(p):
        for j in range(1, M):
            to = lax.rem(m + j, M)
            for i in range(D):
                zs[p, j - 1, i] = g[i * S + s, :, columns(p * pw + to * zw, zw)].astype(BF16)
        flying[p] = [
            send(zs.at[p, j - 1], zr.at[p, j - 1], (s, d, lax.rem(m + j, M)))
            for j in range(1, M)
        ]

    def group_take(p):
        for copy in flying[p]:
            copy.wait_recv()
        for i in range(D):
            total = g[i * S + s, :, columns(p * pw + m * zw, zw)]
            for j in range(M - 1):
                total = total + zr[p, j, i].astype(F32)
            fin[p, i] = total.astype(BF16)
        flying[p] = []
        for i, j in others:
            to = lax.rem(d + i, D)
            flying[p].append(
                send(fin.at[p, to], fr.at[p, d * M + m], (s, to, lax.rem(m + j, M)))
            )
        fr[p, d * M + m] = fin[p, d]

    def finish(p):
        for copy in flying[p]:
            copy.wait_recv()
        for i in range(D):
            for j in range(M):
                at = i * cw + p * pw + j * zw
                gimg_ref[:, at : at + zw] = fr[p, i * M + j].astype(F32)

    for p in range(parts):
        halve_send(0, p)
    adapter_up()
    stages = []
    for n in range(1, len(ladder)):
        stages.append(lambda p, n=n: (halve_take(n - 1, p), halve_send(n, p)))
    stages.append(lambda p: (halve_take(len(ladder) - 1, p), group_send(p)))
    stages.append(group_take)
    stages.append(finish)
    for t in range(parts + len(stages) - 1):
        for k, stage in enumerate(stages):
            if 0 <= t - k < parts:
                stage(t - k)
        if t == parts - 1:
            adapter_down()
    for copy in started:
        copy.wait_send()


def deliver(x0, x1, x2, y0, y1, y2, sems):
    copies = [
        pltpu.make_async_copy(x, y, sems.at[i])
        for i, (x, y) in enumerate([(x0, y0), (x1, y1), (x2, y2)])
    ]
    for copy in copies:
        copy.start()
    for copy in copies:
        copy.wait()


def body(
    encoder_image_states,
    frozen_key_value,
    adapter_down_weight,
    adapter_up_weight,
    queries,
    cotangent,
    text_token_length,
    image_tile_count,
    *,
    sizes,
):
    S, D, M = sizes
    rows_loc, width = encoder_image_states.shape[1:]
    cw, kvc = frozen_key_value.shape[1], frozen_key_value.shape[3]
    qw, ranks = adapter_down_weight.shape[1:]
    text, qcols = queries.shape[2:]
    nb = S * D
    rows, srows = nb * rows_loc, S * rows_loc
    parts = max(1, min(2, cw // M // 128))
    pw = cw // parts
    zw = pw // M
    vmem = pl.BlockSpec(memory_space=pltpu.VMEM)
    smem = pl.BlockSpec(memory_space=pltpu.SMEM)
    hbm = pl.BlockSpec(memory_space=pl.ANY)
    halves = []
    bits = bits_down(S)
    for b in reversed(bits):
        halves += [pltpu.VMEM((parts, D * S // (2 * b), rows_loc, pw), BF16)] * 2
    sends = (nb - 1) + (S - 1) + (M - 1) + 4 * (D - 1) + (D * M - 1)
    sends += parts * (len(bits) + (M - 1) + (D * M - 1))
    shapes = (
        jax.ShapeDtypeStruct((qw, ranks), BF16),
        jax.ShapeDtypeStruct(adapter_up_weight.shape[1:], BF16),
        jax.ShapeDtypeStruct((rows_loc, width), F32),
    )
    down, up, image = pl.pallas_call(
        functools.partial(kernel, sizes, parts),
        out_shape=shapes,
        in_specs=[smem, smem, hbm, vmem, hbm, hbm, hbm, hbm],
        out_specs=(vmem, vmem, vmem),
        scratch_shapes=[
            pltpu.VMEM((cw, 2 * kvc), BF16),
            pltpu.VMEM((qw, ranks), BF16),
            pltpu.VMEM((text, qcols), BF16),
            pltpu.VMEM((text, qcols), BF16),
            pltpu.VMEM((nb, rows_loc, cw), BF16),
            pltpu.VMEM((D, S, rows_loc, qw), BF16),
            pltpu.VMEM((srows, ranks), F32),
            pltpu.VMEM((M, srows, ranks), F32),
            pltpu.VMEM((D, srows, ranks), BF16),
            pltpu.VMEM((D, srows, 2 * kvc), F32),
            pltpu.VMEM((D, srows, 2 * kvc), F32),
            pltpu.VMEM((srows, 2 * kvc), BF16),
            pltpu.VMEM((D, srows, 2 * kvc), BF16),
            pltpu.VMEM((srows, ranks), F32),
            pltpu.VMEM((D, M, srows, ranks), F32),
            pltpu.VMEM((nb, rows_loc, cw), F32),
            pltpu.VMEM((parts, M - 1, D, rows_loc, zw), BF16),
            pltpu.VMEM((parts, M - 1, D, rows_loc, zw), BF16),
            pltpu.VMEM((parts, D, rows_loc, zw), BF16),
            pltpu.VMEM((parts, D * M, rows_loc, zw), BF16),
            pltpu.SemaphoreType.DMA((6,)),
            pltpu.SemaphoreType.DMA((sends,)),
            pltpu.SemaphoreType.DMA((sends,)),
            *halves,
        ],
        compiler_params=pltpu.CompilerParams(
            collective_id=0, has_side_effects=True, vmem_limit_bytes=58 * 2**20
        ),
    )(
        text_token_length,
        image_tile_count,
        encoder_image_states[0],
        adapter_up_weight[0],
        frozen_key_value[0].reshape(cw, 2 * kvc),
        adapter_down_weight[0],
        queries[0, 0],
        cotangent[0, 0],
    )
    down, up, image = pl.pallas_call(
        deliver,
        out_shape=shapes,
        in_specs=[hbm] * 3,
        out_specs=(hbm,) * 3,
        scratch_shapes=[pltpu.SemaphoreType.DMA((3,))],
        compiler_params=pltpu.CompilerParams(vmem_limit_bytes=58 * 2**20),
    )(down, up, image)
    return down[None], up[None], image[None]


def solution(mesh):
    in_specs = (
        P("dp", "segment", None),
        P("segment", "dp", None, "mp"),
        P("segment", "mp", None),
        P("segment", None, None, "mp"),
        P("segment", "dp", None, "mp"),
        P("segment", "dp", None, "mp"),
        P("dp"),
        P("dp"),
    )
    out_specs = (P("segment", "mp", None), P("segment", None, None, "mp"), P("dp", "segment", None))
    sizes = (mesh.shape["segment"], mesh.shape["dp"], mesh.shape["mp"])
    return jax.shard_map(
        functools.partial(body, sizes=sizes),
        mesh=mesh, in_specs=in_specs, out_specs=out_specs, check_vma=False,
    )
```

time: 57 us -> 74.5 us (1.31)
  Pallas kernels: 44.9 us -> 67.5 us
  local copies, waits for them, and re-layouts: 9.87 us -> 4.85 us
    pallas_call x1 -> x2, Pallas kernels: 44.9 us -> 67.5 us  [the longest x1 40.6 us: body(): pl.pallas_call(functools.partial(kernel, sizes, parts), out_shape=shapes,...]
    unnamed x4 -> x1, local copies, waits for them, and re-layouts: 9.87 us -> 4.85 us
where the time goes in v2:
time: 74.5 us; the launch traced here: 74.3 us
  Pallas kernels  67.5 us (91%)
  local copies, waits for them, and re-layouts  4.85 us (7%)
  between operations  1.93 us (3%)
    pallas_call x1, Pallas kernels, body(): pl.pallas_call(functools.partial(kernel, sizes, parts), out_shape=shapes,...  40.6 us
    pallas_call x1, Pallas kernels, body(): pl.pallas_call(deliver, out_shape=shapes, in_specs=[hbm] * 3, out_specs=(...  26.9 us
    unnamed x1, local copies, waits for them, and re-layouts  4.85 us

profile of v2, /device:TPU:0, one launch (start us, length us, event | category | flops | bytes accessed | tf_op | source)
XLA Modules:
  0.0 74.3 jit_solution(16907952627480977440)
XLA Ops:
  1.9 4.9 %copy.11 = bf16[512,8,2,256]{3,1,2,0:T(8,128)(2,1)} copy(bf16[512,8,2,256]{3,2,1,0:T(2,128)(2,1)} %bitcast.12) | data formatting | bytes 8388608
  6.8 40.6 %shard_map.103 = (bf16[2048,128]{1,0:T(8,128)(2,1)}, bf16[2,64,256]{2,1,0:T(8,128)(2,1)}, f32[8,8192]{1,0:T(8,128)}) custom-call(s32[1]{0:T(128)S(6)} %copy.12.len_ref, s32[1]{0:T(128)S(6)} %copy.13.tiles_ref, bf16[8,8192]{1,0:T(8,128)(2,1)} %bitcast.16, bf16[2,64,256]{2,1,0:T(8,128)(2,1)} %bitcast.17, bf16[4096,512]{1,0:T(8,128)(2,1)} %bitcast.11, ...), custom_call_target="tpu_custom_call" | custom-call | tf_op jit(solution)/shard_map/pallas_call | solution.py:350
  47.4 26.9 %shard_map.104 = (bf16[2048,128]{1,0:T(8,128)(2,1)}, bf16[2,64,256]{2,1,0:T(8,128)(2,1)}, f32[8,8192]{1,0:T(8,128)}) custom-call(bf16[2048,128]{1,0:T(8,128)(2,1)} %get-tuple-element.9.x0, bf16[2,64,256]{2,1,0:T(8,128)(2,1)} %get-tuple-element.10.x1, f32[8,8192]{1,0:T(8,128)} %get-tuple-element.11.x2), custom_call_target="tpu_custom_call" | custom-call | tf_op jit(solution)/shard_map/pallas_call | solution.py:394

commit v3 on v2

--- a/solution.py
+++ b/solution.py
@@ -37,7 +37,7 @@
     sizes, parts,
     len_ref, tiles_ref, img_ref, up_ref, w_hbm, a_hbm, q_hbm, c_hbm,
     gdown_ref, gup_ref, gimg_ref,
-    w, a, q, c, xh, xq, low_p, low_r, low_b, kv_p, kv_r, dkv_own, dkv, back_p, back_r,
+    raw, w, a, q, c, xh, xq, low_p, low_r, low_b, kv_p, kv_r, dkv_own, dkv, back_p, back_r,
     g, zs, zr, fin, fr, load_sem, send_sem, recv_sem, *halves,
 ):
     S, D, M = sizes
@@ -63,13 +63,13 @@
                 (img_ref.at[:, columns(d * cw, cw)], xh.at[d * S + s]),
                 (img_ref.at[:, columns(m * qw, qw)], xq.at[d, s]),
                 (a_hbm, a),
-                (w_hbm, w),
                 (q_hbm, q),
                 (c_hbm, c),
             ]
+            + [(w_hbm.at[:, :, j * HD : (j + 1) * HD], raw.at[j]) for j in range(kvc // HD)]
         )
     ]
-    for load in loads:
+    for load in loads[5:] + loads[:5]:
         load.start()
 
     others = [(i, j) for i in range(D) for j in range(M) if i or j]
@@ -97,6 +97,23 @@
     def across(step, at):
         kind, b = step
         return (at[0], flip(at[1], b)) if kind == "d" else (flip(at[0], b), at[1])
+
+    block = 128
+    place = lax.broadcasted_iota(jnp.int32, (2 * block, 2 * block), 0)
+    source = lax.broadcasted_iota(jnp.int32, (2 * block, 2 * block), 1)
+    apart = jnp.where(
+        source == jnp.where(place < block, 2 * place, 2 * (place - block) + 1), 1.0, 0.0
+    ).astype(BF16)
+
+    def separate(i, carry):
+        at = pl.ds(pl.multiple_of(i * block, block), block)
+        pairs = jnp.concatenate(
+            [raw[j, at].reshape(2 * block, HD) for j in range(kvc // HD)], axis=1
+        )
+        sorted_rows = dot(apart, pairs, NN).astype(BF16)
+        w[at, :kvc] = sorted_rows[:block]
+        w[at, kvc:] = sorted_rows[block:]
+        return carry
 
     me = (s, d)
     held = [[] for _ in steps]
@@ -107,7 +124,13 @@
         if step[0] == "s":
             quarter = img_ref.at[:, columns(m * qw, qw)]
             held[k].append((send(quarter, xq.at[d, s], (*to, m)), "quarter", to))
+    for load in loads[5:]:
+        load.wait()
+    blocks = cw // block
     for k in range(len(steps)):
+        lax.fori_loop(
+            blocks * k // len(steps), blocks * (k + 1) // len(steps), separate, 0
+        )
         for copy, kind, at in list(held[k]):
             copy.wait_recv()
             slot = xh.at[at[1] * S + at[0]] if kind == "half" else xq.at[d, at[0]]
@@ -129,12 +152,13 @@
     low_r[m] = low_p[...]
 
     xall = xh[...].astype(F32).reshape(rows, cw).astype(BF16)
-    loads[3].wait()
-    kv_p[...] = dot(xall, w[...], NN).reshape(kv_p.shape)
     samples = [lax.rem(d + i, D) for i in range(1, D)]
-    kv_c = [send(kv_p.at[to], kv_r.at[d], (s, to, m)) for to in samples]
+    kv_c = []
+    for n in range(2):
+        kv_p[n] = dot(xall, w[:, n * kvc : (n + 1) * kvc], NN).reshape(D, srows, kvc)
+        kv_c += [send(kv_p.at[n, to], kv_r.at[n, d], (s, to, m)) for to in samples]
+        kv_r[n, d] = kv_p[n, d]
     xq_c = [send(xq.at[d], xq.at[d], (s, to, m)) for to in samples]
-    kv_r[d] = kv_p[d]
     for copy in low_c:
         copy.wait_recv()
     low_own = jnp.sum(low_r[...], axis=0).astype(BF16)
@@ -143,10 +167,11 @@
     adapted = jnp.concatenate([dot(low_own, ukk, NN), dot(low_own, uvv, NN)], axis=1)
     for copy in kv_c:
         copy.wait_recv()
-    kv = (jnp.sum(kv_r[...], axis=0) + ADAPTER_SCALE * adapted).astype(BF16)
-
+    frozen = jnp.concatenate([jnp.sum(kv_r[0], axis=0), jnp.sum(kv_r[1], axis=0)], axis=1)
+    kv = (frozen + ADAPTER_SCALE * adapted).astype(BF16)
+
+    loads[3].wait()
     loads[4].wait()
-    loads[5].wait()
     text = q.shape[0]
     heads = q.shape[1] // HD
     kv_heads = kvc // HD
@@ -340,7 +365,7 @@
     bits = bits_down(S)
     for b in reversed(bits):
         halves += [pltpu.VMEM((parts, D * S // (2 * b), rows_loc, pw), BF16)] * 2
-    sends = (nb - 1) + (S - 1) + (M - 1) + 4 * (D - 1) + (D * M - 1)
+    sends = (nb - 1) + (S - 1) + (M - 1) + 5 * (D - 1) + (D * M - 1)
     sends += parts * (len(bits) + (M - 1) + (D * M - 1))
     shapes = (
         jax.ShapeDtypeStruct((qw, ranks), BF16),
@@ -353,6 +378,7 @@
         in_specs=[smem, smem, hbm, vmem, hbm, hbm, hbm, hbm],
         out_specs=(vmem, vmem, vmem),
         scratch_shapes=[
+            pltpu.VMEM((kvc // HD, cw, 2, HD), BF16),
             pltpu.VMEM((cw, 2 * kvc), BF16),
             pltpu.VMEM((qw, ranks), BF16),
             pltpu.VMEM((text, qcols), BF16),
@@ -362,8 +388,8 @@
             pltpu.VMEM((srows, ranks), F32),
             pltpu.VMEM((M, srows, ranks), F32),
             pltpu.VMEM((D, srows, ranks), BF16),
-            pltpu.VMEM((D, srows, 2 * kvc), F32),
-            pltpu.VMEM((D, srows, 2 * kvc), F32),
+            pltpu.VMEM((2, D, srows, kvc), F32),
+            pltpu.VMEM((2, D, srows, kvc), F32),
             pltpu.VMEM((srows, 2 * kvc), BF16),
             pltpu.VMEM((D, srows, 2 * kvc), BF16),
             pltpu.VMEM((srows, ranks), F32),
@@ -373,7 +399,7 @@
             pltpu.VMEM((parts, M - 1, D, rows_loc, zw), BF16),
             pltpu.VMEM((parts, D, rows_loc, zw), BF16),
             pltpu.VMEM((parts, D * M, rows_loc, zw), BF16),
-            pltpu.SemaphoreType.DMA((6,)),
+            pltpu.SemaphoreType.DMA((5 + kvc // HD,)),
             pltpu.SemaphoreType.DMA((sends,)),
             pltpu.SemaphoreType.DMA((sends,)),
             *halves,
@@ -386,7 +412,7 @@
         image_tile_count,
         encoder_image_states[0],
         adapter_up_weight[0],
-        frozen_key_value[0].reshape(cw, 2 * kvc),
+        frozen_key_value[0],
         adapter_down_weight[0],
         queries[0, 0],
         cotangent[0, 0],
@@ -394,10 +420,9 @@
     down, up, image = pl.pallas_call(
         deliver,
         out_shape=shapes,
-        in_specs=[hbm] * 3,
+        in_specs=[vmem] * 3,
         out_specs=(hbm,) * 3,
         scratch_shapes=[pltpu.SemaphoreType.DMA((3,))],
-        compiler_params=pltpu.CompilerParams(vmem_limit_bytes=58 * 2**20),
     )(down, up, image)
     return down[None], up[None], image[None]
 

time: 74.5 us -> 46.5 us (0.62)
  Pallas kernels: 67.5 us -> 44.3 us
  local copies, waits for them, and re-layouts: 4.85 us -> 0 us
    pallas_call x1, Pallas kernels: 26.9 us -> 2.07 us  [body(): pl.pallas_call(deliver, out_shape=shapes, in_specs=[vmem] * 3, out_specs=...]
    unnamed x1 -> x0, local copies, waits for them, and re-layouts: 4.85 us -> none
    pallas_call x1, Pallas kernels: 40.6 us -> 42.3 us  [body(): pl.pallas_call(functools.partial(kernel, sizes, parts), out_shape=shapes,...]
where the time goes in v3:
time: 46.5 us; the launch traced here: 46.3 us
  Pallas kernels  44.3 us (95%)
  between operations  1.93 us (4%)
    pallas_call x1, Pallas kernels, body(): pl.pallas_call(functools.partial(kernel, sizes, parts), out_shape=shapes,...  42.3 us
    pallas_call x1, Pallas kernels, body(): pl.pallas_call(deliver, out_shape=shapes, in_specs=[vmem] * 3, out_specs=...  2.07 us

profile of v3, /device:TPU:0, one launch (start us, length us, event | category | flops | bytes accessed | tf_op | source)
XLA Modules:
  0.0 46.3 jit_solution(9982081380678058861)
XLA Ops:
  1.9 42.3 %shard_map.103 = (bf16[2048,128]{1,0:T(8,128)(2,1)}, bf16[2,64,256]{2,1,0:T(8,128)(2,1)}, f32[8,8192]{1,0:T(8,128)}) custom-call(s32[1]{0:T(128)S(6)} %copy.11.len_ref, s32[1]{0:T(128)S(6)} %copy.12.tiles_ref, bf16[8,8192]{1,0:T(8,128)(2,1)} %bitcast.13, bf16[2,64,256]{2,1,0:T(8,128)(2,1)} %bitcast.14, bf16[4096,2,256]{2,1,0:T(2,128)(2,1)} %bitcast.9, ...), custom_call_target="tpu_custom_call" | custom-call | tf_op jit(solution)/shard_map/pallas_call | solution.py:375
  44.2 2.1 %shard_map.104 = (bf16[2048,128]{1,0:T(8,128)(2,1)}, bf16[2,64,256]{2,1,0:T(8,128)(2,1)}, f32[8,8192]{1,0:T(8,128)}) custom-call(bf16[2048,128]{1,0:T(8,128)(2,1)} %get-tuple-element.9.x0, bf16[2,64,256]{2,1,0:T(8,128)(2,1)} %get-tuple-element.10.x1, f32[8,8192]{1,0:T(8,128)} %get-tuple-element.11.x2), custom_call_target="tpu_custom_call" | custom-call | tf_op jit(solution)/shard_map/pallas_call | solution.py:420

commit v4 on v3

--- a/solution.py
+++ b/solution.py
@@ -35,10 +35,10 @@
 
 def kernel(
     sizes, parts,
-    len_ref, tiles_ref, img_ref, up_ref, w_hbm, a_hbm, q_hbm, c_hbm,
-    gdown_ref, gup_ref, gimg_ref,
-    raw, w, a, q, c, xh, xq, low_p, low_r, low_b, kv_p, kv_r, dkv_own, dkv, back_p, back_r,
-    g, zs, zr, fin, fr, load_sem, send_sem, recv_sem, *halves,
+    len_ref, tiles_ref, img_ref, up_hbm, w_hbm, a_hbm, q_hbm, c_hbm,
+    gdown_hbm, gup_hbm, gimg_hbm,
+    up_ref, gdown_ref, gup_ref, raw, w, a, q, c, xh, xq, low_p, low_r, low_b, kv_p, kv_r, dkv_own, dkv, back_p, back_r,
+    g, zs, zr, fin, fr, load_sem, store_sem, send_sem, recv_sem, *halves,
 ):
     S, D, M = sizes
     s, d, m = lax.axis_index("segment"), lax.axis_index("dp"), lax.axis_index("mp")
@@ -65,11 +65,12 @@
                 (a_hbm, a),
                 (q_hbm, q),
                 (c_hbm, c),
+                (up_hbm, up_ref),
             ]
             + [(w_hbm.at[:, :, j * HD : (j + 1) * HD], raw.at[j]) for j in range(kvc // HD)]
         )
     ]
-    for load in loads[5:] + loads[:5]:
+    for load in loads[6:] + loads[:6]:
         load.start()
 
     others = [(i, j) for i in range(D) for j in range(M) if i or j]
@@ -124,7 +125,7 @@
         if step[0] == "s":
             quarter = img_ref.at[:, columns(m * qw, qw)]
             held[k].append((send(quarter, xq.at[d, s], (*to, m)), "quarter", to))
-    for load in loads[5:]:
+    for load in loads[6:]:
         load.wait()
     blocks = cw // block
     for k in range(len(steps)):
@@ -140,6 +141,7 @@
                     (send(slot, slot, (*to, m)), kind, across(steps[later], at))
                 )
 
+    loads[5].wait()
     ukk = jnp.concatenate([up_ref[0], jnp.zeros_like(up_ref[0])], axis=0)
     uvv = jnp.concatenate([jnp.zeros_like(up_ref[1]), up_ref[1]], axis=0)
 
@@ -239,12 +241,14 @@
         rank = low.shape[1] // 2
         gup_ref[0] = (ADAPTER_SCALE * dot(low, dall[:, :kvc], TN)[:rank]).astype(BF16)
         gup_ref[1] = (ADAPTER_SCALE * dot(low, dall[:, kvc:], TN)[rank:]).astype(BF16)
+        store(gup_ref, gup_hbm)
 
     def adapter_down():
         for copy in xq_c:
             copy.wait_recv()
         all_q = xq[...].astype(F32).reshape(rows, qw).astype(BF16)
         gdown_ref[...] = dot(all_q, back, TN).astype(BF16)
+        store(gdown_ref, gdown_hbm)
 
     ladder = list(reversed(s_bits))
     flying = {}
@@ -298,17 +302,20 @@
             )
         fr[p, d * M + m] = fin[p, d]
 
+    stores = []
+
+    def store(src, dst):
+        copy = pltpu.make_async_copy(src, dst, store_sem.at[len(stores)])
+        copy.start()
+        stores.append(copy)
+
     def finish(p):
         for copy in flying[p]:
             copy.wait_recv()
-        for i in range(D):
-            for j in range(M):
-                at = i * cw + p * pw + j * zw
-                gimg_ref[:, at : at + zw] = fr[p, i * M + j].astype(F32)
+        store(fr.at[p], gimg_hbm.at[p])
 
     for p in range(parts):
         halve_send(0, p)
-    adapter_up()
     stages = []
     for n in range(1, len(ladder)):
         stages.append(lambda p, n=n: (halve_take(n - 1, p), halve_send(n, p)))
@@ -317,21 +324,33 @@
     stages.append(finish)
     for t in range(parts + len(stages) - 1):
         for k, stage in enumerate(stages):
+            if k == len(stages) - 1 and t == parts + k - 2:
+                adapter_down()
             if 0 <= t - k < parts:
                 stage(t - k)
-        if t == parts - 1:
-            adapter_down()
+            if k == 0 and t == min(1, parts - 1):
+                adapter_up()
+    for copy in stores:
+        copy.wait()
     for copy in started:
         copy.wait_send()
 
 
-def deliver(x0, x1, x2, y0, y1, y2, sems):
+def deliver(sizes, parts, x0, x1, x2, y0, y1, y2, wide, sems):
+    D, M = sizes
+    zw = x2.shape[3]
     copies = [
         pltpu.make_async_copy(x, y, sems.at[i])
-        for i, (x, y) in enumerate([(x0, y0), (x1, y1), (x2, y2)])
+        for i, (x, y) in enumerate([(x0, y0), (x1, y1), (wide, y2)])
     ]
-    for copy in copies:
-        copy.start()
+    copies[0].start()
+    copies[1].start()
+    for i in range(D):
+        for p in range(parts):
+            for j in range(M):
+                at = ((i * parts + p) * M + j) * zw
+                wide[:, at : at + zw] = x2[p, i * M + j].astype(F32)
+    copies[2].start()
     for copy in copies:
         copy.wait()
 
@@ -355,7 +374,7 @@
     text, qcols = queries.shape[2:]
     nb = S * D
     rows, srows = nb * rows_loc, S * rows_loc
-    parts = max(1, min(2, cw // M // 128))
+    parts = max(1, min(4, cw // M // 128))
     pw = cw // parts
     zw = pw // M
     vmem = pl.BlockSpec(memory_space=pltpu.VMEM)
@@ -374,10 +393,13 @@
     )
     down, up, image = pl.pallas_call(
         functools.partial(kernel, sizes, parts),
-        out_shape=shapes,
-        in_specs=[smem, smem, hbm, vmem, hbm, hbm, hbm, hbm],
-        out_specs=(vmem, vmem, vmem),
+        out_shape=(*shapes[:2], jax.ShapeDtypeStruct((parts, D * M, rows_loc, zw), BF16)),
+        in_specs=[smem, smem] + [hbm] * 6,
+        out_specs=(hbm, hbm, hbm),
         scratch_shapes=[
+            pltpu.VMEM(adapter_up_weight.shape[1:], BF16),
+            pltpu.VMEM((qw, ranks), BF16),
+            pltpu.VMEM(adapter_up_weight.shape[1:], BF16),
             pltpu.VMEM((kvc // HD, cw, 2, HD), BF16),
             pltpu.VMEM((cw, 2 * kvc), BF16),
             pltpu.VMEM((qw, ranks), BF16),
@@ -399,7 +421,8 @@
             pltpu.VMEM((parts, M - 1, D, rows_loc, zw), BF16),
             pltpu.VMEM((parts, D, rows_loc, zw), BF16),
             pltpu.VMEM((parts, D * M, rows_loc, zw), BF16),
-            pltpu.SemaphoreType.DMA((5 + kvc // HD,)),
+            pltpu.SemaphoreType.DMA((6 + kvc // HD,)),
+            pltpu.SemaphoreType.DMA((2 + parts,)),
             pltpu.SemaphoreType.DMA((sends,)),
             pltpu.SemaphoreType.DMA((sends,)),
             *halves,
@@ -418,11 +441,11 @@
         cotangent[0, 0],
     )
     down, up, image = pl.pallas_call(
-        deliver,
+        functools.partial(deliver, (D, M), parts),
         out_shape=shapes,
         in_specs=[vmem] * 3,
         out_specs=(hbm,) * 3,
-        scratch_shapes=[pltpu.SemaphoreType.DMA((3,))],
+        scratch_shapes=[pltpu.VMEM((rows_loc, width), F32), pltpu.SemaphoreType.DMA((3,))],
     )(down, up, image)
     return down[None], up[None], image[None]
 

time: 46.5 us -> 50.8 us (1.092)
  Pallas kernels: 44.3 us -> 48.7 us
    pallas_call x2, Pallas kernels: 44.3 us -> 48.7 us  [the longest x1 46.7 us: body(): pl.pallas_call(functools.partial(kernel, sizes, parts), out_shape=(*shape...]
where the time goes in v4:
time: 50.8 us; the launch traced here: 50.6 us
  Pallas kernels  48.7 us (96%)
  between operations  1.93 us (4%)
    pallas_call x1, Pallas kernels, body(): pl.pallas_call(functools.partial(kernel, sizes, parts), out_shape=(*shape...  46.7 us
    pallas_call x1, Pallas kernels, body(): pl.pallas_call(functools.partial(deliver, (D, M), parts), out_shape=shape...  2.02 us

profile of v4, /device:TPU:0, one launch (start us, length us, event | category | flops | bytes accessed | tf_op | source)
XLA Modules:
  0.0 50.6 jit_solution(13382704823926957558)
XLA Ops:
  1.9 46.7 %shard_map.103 = (bf16[2048,128]{1,0:T(8,128)(2,1)}, bf16[2,64,256]{2,1,0:T(8,128)(2,1)}, bf16[4,8,8,256]{3,2,1,0:T(8,128)(2,1)}) custom-call(s32[1]{0:T(128)S(6)} %copy.11.len_ref, s32[1]{0:T(128)S(6)} %copy.12.tiles_ref, bf16[8,8192]{1,0:T(8,128)(2,1)} %bitcast.13, bf16[2,64,256]{2,1,0:T(8,128)(2,1)} %bitcast.14, bf16[4096,2,256]{2,1,0:T(2,128)(2,1)} %bitcast.9, ...), custom_call_target="tpu_custom_call" | custom-call | tf_op jit(solution)/shard_map/pallas_call | solution.py:394
  48.6 2.0 %shard_map.104 = (bf16[2048,128]{1,0:T(8,128)(2,1)}, bf16[2,64,256]{2,1,0:T(8,128)(2,1)}, f32[8,8192]{1,0:T(8,128)}) custom-call(bf16[2048,128]{1,0:T(8,128)(2,1)} %get-tuple-element.9.x0, bf16[2,64,256]{2,1,0:T(8,128)(2,1)} %get-tuple-element.10.x1, bf16[4,8,8,256]{3,2,1,0:T(8,128)(2,1)} %get-tuple-element.11.x2), custom_call_target="tpu_custom_call" | custom-call | tf_op jit(solution)/shard_map/pallas_call | solution.py:443

commit v5 on v4

--- a/solution.py
+++ b/solution.py
@@ -374,7 +374,7 @@
     text, qcols = queries.shape[2:]
     nb = S * D
     rows, srows = nb * rows_loc, S * rows_loc
-    parts = max(1, min(4, cw // M // 128))
+    parts = max(1, min(2, cw // M // 128))
     pw = cw // parts
     zw = pw // M
     vmem = pl.BlockSpec(memory_space=pltpu.VMEM)

time: 50.8 us -> 45 us (0.89)
  Pallas kernels: 48.7 us -> 42.9 us
    pallas_call x1, Pallas kernels: 46.7 us -> 40.9 us  [body(): pl.pallas_call(functools.partial(kernel, sizes, parts), out_shape=(*shape...]
where the time goes in v5:
time: 45 us; the launch traced here: 44.8 us
  Pallas kernels  42.9 us (95%)
  between operations  1.93 us (4%)
    pallas_call x1, Pallas kernels, body(): pl.pallas_call(functools.partial(kernel, sizes, parts), out_shape=(*shape...  40.9 us
    pallas_call x1, Pallas kernels, body(): pl.pallas_call(functools.partial(deliver, (D, M), parts), out_shape=shape...  2.02 us

profile of v5, /device:TPU:0, one launch (start us, length us, event | category | flops | bytes accessed | tf_op | source)
XLA Modules:
  0.0 44.8 jit_solution(16657464183034203423)
XLA Ops:
  1.9 40.9 %shard_map.103 = (bf16[2048,128]{1,0:T(8,128)(2,1)}, bf16[2,64,256]{2,1,0:T(8,128)(2,1)}, bf16[2,8,8,512]{3,2,1,0:T(8,128)(2,1)}) custom-call(s32[1]{0:T(128)S(6)} %copy.11.len_ref, s32[1]{0:T(128)S(6)} %copy.12.tiles_ref, bf16[8,8192]{1,0:T(8,128)(2,1)} %bitcast.13, bf16[2,64,256]{2,1,0:T(8,128)(2,1)} %bitcast.14, bf16[4096,2,256]{2,1,0:T(2,128)(2,1)} %bitcast.9, ...), custom_call_target="tpu_custom_call" | custom-call | tf_op jit(solution)/shard_map/pallas_call | solution.py:394
  42.8 2.0 %shard_map.104 = (bf16[2048,128]{1,0:T(8,128)(2,1)}, bf16[2,64,256]{2,1,0:T(8,128)(2,1)}, f32[8,8192]{1,0:T(8,128)}) custom-call(bf16[2048,128]{1,0:T(8,128)(2,1)} %get-tuple-element.9.x0, bf16[2,64,256]{2,1,0:T(8,128)(2,1)} %get-tuple-element.10.x1, bf16[2,8,8,512]{3,2,1,0:T(8,128)(2,1)} %get-tuple-element.11.x2), custom_call_target="tpu_custom_call" | custom-call | tf_op jit(solution)/shard_map/pallas_call | solution.py:443
